TPU v7x, 32 devices: a whole 2x2x4 slice. The times are simulated.
32 devices in a mesh: tm: 4 (over z), space: 8 (over y, x, core).
Axes of the slice: x: 2, y: 2, z: 4, core: 2. Of those that a mesh axis runs over, the one named last changes fastest.
Arguments:
- noise_field: float32 [8, 4, 8, 6, 256], P(None, 'tm', 'space'), may hold values from -6 to 6
- gauge_links: float32 [4, 3, 4, 8, 6, 256], P(None, None, 'tm', 'space'), may hold values from -2.5 to 2.5
- clover: float32 [2, 6, 4, 8, 12, 256], P(None, None, 'tm', 'space'), may hold values from -0.9 to 0.9
- eigvecs: float32 [48, 4, 8, 6, 256], P(None, 'tm', 'space'), may hold values from -0.0546875 to 0.0546875
- partner: int32 [48], replicated, may hold values from 0 to 47, each once
- dilution: int32 [8], replicated, may hold values from 0 to 3
- boundary: int32 [4], replicated, may hold values from 0 to 1
Outputs:
- perambulator: float32 [32, 4, 96], P('space', 'tm')
- correlator: float32 [32, 4, 4], P('space', 'tm')
Inputs may be any that keep to these rules, and one draw needn't show every extreme that they name: `partner`: each of 0 to 47 once.
All inputs are finite; a program needn't handle non-finite values.
Results may differ from a plain program's by a relative error of at most 0.00029.
Values sent between devices are 32-bit elements; how exact they have to be, the bound alone decides.
A program may use at most 64 MiB of HBM per device.

v0:
```python
import jax
import jax.numpy as jnp
from jax import lax
from jax.sharding import PartitionSpec as P

ITERS = 4
DILUTE = 4
SIDE = 16


diag_term = 4.1
step_size = 0.2
twist_table = (
    (((1, 0, -1), (0, 0, -1)), ((1, 0, 1), (0, 0, 1))),
    (((1, -1, 0), (0, 1, 0)), ((1, 1, 0), (0, -1, 0))),
    (((0, 0, -1), (1, 0, 1)), ((0, 0, 1), (1, 0, -1))),
    (((0, 1, 0), (1, 1, 0)), ((0, 1, 0), (1, 1, 0))),
)


def padded(array, sides, width):
    for axis, dim in sides:
        size, length = (lax.axis_size(axis), array.shape[dim])
        up = [(i, (i + 1) % size) for i in range(size)]
        down = [(j, i) for i, j in up]
        last = lax.slice_in_dim(array, length - width, length, axis=dim)
        initial = lax.slice_in_dim(array, 0, width, axis=dim)
        before = lax.ppermute(last, axis, up)
        after = lax.ppermute(initial, axis, down)
        array = jnp.concatenate([before, array, after], axis=dim)
    return array


def pair_add(first_pair, second_pair):
    return (first_pair[0] + second_pair[0], first_pair[1] + second_pair[1])


def pair_sub(first_pair, second_pair):
    return (first_pair[0] - second_pair[0], first_pair[1] - second_pair[1])


def pair_scale(factor, value_pair):
    return (factor * value_pair[0], factor * value_pair[1])


def pair_map(function_one, value_pair):
    return (function_one(value_pair[0]), function_one(value_pair[1]))


def scaled(value_pair, real_coef, imag_coef):
    if imag_coef == 0:
        return (real_coef * value_pair[0], real_coef * value_pair[1])
    return (-imag_coef * value_pair[1], imag_coef * value_pair[0])


def spin_twist(direction, adjoint, half_pair):
    outputs = []
    for source_spin, real_coef, imag_coef in twist_table[direction][adjoint]:
        picked = (half_pair[0][:, source_spin], half_pair[1][:, source_spin])
        outputs.append(scaled(picked, real_coef, imag_coef))
    return (
        jnp.stack([outputs[0][0], outputs[1][0]], 1),
        jnp.stack([outputs[0][1], outputs[1][1]], 1),
    )


def split_spins(spinor_pair):
    upper_half = (spinor_pair[0][:, 0:2], spinor_pair[1][:, 0:2])
    lower_half = (spinor_pair[0][:, 2:4], spinor_pair[1][:, 2:4])
    return (upper_half, lower_half)


def link_apply(link_real, link_imag, half_pair):
    total_real = 0.0
    total_imag = 0.0
    for column in range(3):
        matrix_real = jnp.moveaxis(link_real[:, :, :, column, :], 0, 2)
        matrix_imag = jnp.moveaxis(link_imag[:, :, :, column, :], 0, 2)
        vector_real = half_pair[0][..., column : column + 1, :]
        vector_imag = half_pair[1][..., column : column + 1, :]
        total_real = total_real + matrix_real * vector_real - matrix_imag * vector_imag
        total_imag = total_imag + matrix_real * vector_imag + matrix_imag * vector_real
    return (total_real, total_imag)


def link_adjoint(link_real, link_imag, half_pair):
    total_real = 0.0
    total_imag = 0.0
    for matrix_row in range(3):
        matrix_real = link_real[matrix_row]
        matrix_imag = link_imag[matrix_row]
        vector_real = half_pair[0][..., matrix_row : matrix_row + 1, :]
        vector_imag = half_pair[1][..., matrix_row : matrix_row + 1, :]
        total_real = total_real + matrix_real * vector_real + matrix_imag * vector_imag
        total_imag = total_imag + matrix_real * vector_imag - matrix_imag * vector_real
    return (total_real, total_imag)


def plane_shift(values, direction, forward, edge_sign):
    flat_index = lax.broadcasted_iota(jnp.int32, values.shape, values.ndim - 1)
    if direction == 0:
        coordinate = flat_index % SIDE
        if forward:
            return jnp.where(
                coordinate == SIDE - 1,
                edge_sign * jnp.roll(values, SIDE - 1, axis=-1),
                jnp.roll(values, -1, axis=-1),
            )
        return jnp.where(
            coordinate == 0,
            edge_sign * jnp.roll(values, 1 - SIDE, axis=-1),
            jnp.roll(values, 1, axis=-1),
        )
    coordinate = flat_index // SIDE
    if forward:
        rolled = jnp.roll(values, -SIDE, axis=-1)
        return jnp.where(coordinate == SIDE - 1, edge_sign * rolled, rolled)
    rolled = jnp.roll(values, SIDE, axis=-1)
    return jnp.where(coordinate == 0, edge_sign * rolled, rolled)


def clover_apply(clover, spinor_pair):
    parts_real = []
    parts_imag = []
    for chiral in range(2):
        block_real = clover[chiral][:, :, :, 0::2, :]
        block_imag = clover[chiral][:, :, :, 1::2, :]
        total_real = 0.0
        total_imag = 0.0
        for column in range(6):
            spin_index = 2 * chiral + column // 3
            color_index = column % 3
            vector_real = spinor_pair[0][:, spin_index, :, :, color_index, :][:, None]
            vector_imag = spinor_pair[1][:, spin_index, :, :, color_index, :][:, None]
            entry_real = block_real[:, :, :, column, :]
            entry_imag = block_imag[:, :, :, column, :]
            total_real = total_real + entry_real * vector_real - entry_imag * vector_imag
            total_imag = total_imag + entry_real * vector_imag + entry_imag * vector_real
        counts = total_real.shape
        new_shape = (counts[0], 2, 3) + counts[2:]
        parts_real.append(total_real.reshape(new_shape).transpose(0, 1, 3, 4, 2, 5))
        parts_imag.append(total_imag.reshape(new_shape).transpose(0, 1, 3, 4, 2, 5))
    return (jnp.concatenate(parts_real, 1), jnp.concatenate(parts_imag, 1))


def recombine(direction, ahead_linked, behind_moved):
    top_part = pair_add(ahead_linked, behind_moved)
    bottom_part = pair_sub(
        spin_twist(direction, 1, behind_moved), spin_twist(direction, 1, ahead_linked)
    )
    return (
        jnp.concatenate([top_part[0], bottom_part[0]], 1),
        jnp.concatenate([top_part[1], bottom_part[1]], 1),
    )


def build_source(noise_field, dilution, time_index):
    sources = noise_field.shape[0]
    spin_mask = (
        lax.broadcasted_iota(jnp.int32, (sources, 4), 1)
        == lax.broadcasted_iota(jnp.int32, (sources, 4), 0) % 4
    ).astype(jnp.float32)
    time_mask = (time_index[None, :] % DILUTE == dilution[:, None]).astype(jnp.float32)
    source_weight = (
        spin_mask[:, :, None, None, None, None] * time_mask[:, None, :, None, None, None]
    )
    return (
        source_weight * noise_field[:, None, :, :, 0::2, :],
        source_weight * noise_field[:, None, :, :, 1::2, :],
    )


def project(solution, eigvecs):
    counts = solution[0].shape
    flat_shape = (counts[0] * counts[1], counts[2], counts[3] * counts[4] * counts[5])
    solve_result_real = solution[0].reshape(flat_shape)
    solve_result_imag = solution[1].reshape(flat_shape)
    eig_shape = (eigvecs.shape[0], eigvecs.shape[1], flat_shape[2])
    eigenmode_real = eigvecs[:, :, :, 0::2, :].reshape(eig_shape)
    eigenmode_imag = eigvecs[:, :, :, 1::2, :].reshape(eig_shape)
    highest_value = lax.Precision.HIGHEST
    real_component = jnp.einsum(
        "gdc,xdc->xdg", eigenmode_real, solve_result_real, precision=highest_value
    ) + jnp.einsum("gdc,xdc->xdg", eigenmode_imag, solve_result_imag, precision=highest_value)
    imaginary_component = jnp.einsum(
        "gdc,xdc->xdg", eigenmode_real, solve_result_imag, precision=highest_value
    ) - jnp.einsum("gdc,xdc->xdg", eigenmode_imag, solve_result_real, precision=highest_value)
    return jnp.concatenate([real_component, imaginary_component], 2)


def weigh_pairs(peram_block, partner):
    vectors = partner.shape[0]
    onehot = (partner[:, None] == lax.broadcasted_iota(jnp.int32, (vectors, vectors), 1)).astype(
        jnp.float32
    )
    highest_value = lax.Precision.HIGHEST
    real_component = jnp.einsum(
        "jtk,kl->jtl", peram_block[:, :, :vectors], onehot, precision=highest_value
    )
    imaginary_component = jnp.einsum(
        "jtk,kl->jtl", peram_block[:, :, vectors:], onehot, precision=highest_value
    )
    return jnp.concatenate([real_component, imaginary_component], 2)


def shards(noise_field, gauge_links, clover, eigvecs, partner, dilution, boundary):
    phase_signs = 1.0 - 2.0 * boundary.astype(jnp.float32)
    local_times = noise_field.shape[1]
    local_planes = noise_field.shape[2]
    time_rank = lax.axis_index("tm")
    space_rank = lax.axis_index("space")
    time_index = time_rank * local_times + jnp.arange(local_times, dtype=jnp.int32)
    time_low = jnp.where(time_rank == 0, phase_signs[3], 1.0)
    time_high = jnp.where(time_rank == lax.axis_size("tm") - 1, phase_signs[3], 1.0)
    space_low = jnp.where(space_rank == 0, phase_signs[2], 1.0)
    space_high = jnp.where(space_rank == lax.axis_size("space") - 1, phase_signs[2], 1.0)
    source = build_source(noise_field, dilution, time_index)
    solution = pair_scale(step_size, source)
    for iteration in range(ITERS):
        upper_half, lower_half = split_spins(solution)
        hopping = (0.0, 0.0)
        for direction in range(4):
            link_real = gauge_links[direction][:, :, :, 0::2, :]
            link_imag = gauge_links[direction][:, :, :, 1::2, :]
            if direction < 2:
                twisted = spin_twist(direction, 0, lower_half)
                apply_ahead_half = pair_sub(upper_half, twisted)
                apply_behind_half = link_adjoint(
                    link_real, link_imag, pair_add(upper_half, twisted)
                )
                edge_sign = phase_signs[direction]
                apply_ahead_moved = pair_map(
                    lambda values: plane_shift(values, direction, True, edge_sign), apply_ahead_half
                )
                apply_behind_moved = pair_map(
                    lambda values: plane_shift(values, direction, False, edge_sign),
                    apply_behind_half,
                )
            else:
                twisted = spin_twist(direction, 0, lower_half)
                apply_ahead_half = pair_sub(upper_half, twisted)
                apply_behind_half = link_adjoint(
                    link_real, link_imag, pair_add(upper_half, twisted)
                )
                if direction == 3:
                    time_edge_block = jnp.stack(
                        [
                            jnp.concatenate([apply_ahead_half[0], apply_behind_half[0]], 2),
                            jnp.concatenate([apply_ahead_half[1], apply_behind_half[1]], 2),
                        ]
                    )
                    time_received = padded(time_edge_block, (("tm", 3),), 1)
                    time_from_below = time_received[:, :, :, :1] * time_low
                    time_from_above = time_received[:, :, :, 3:] * time_high
                    time_ahead_moved = (
                        jnp.concatenate([apply_ahead_half[0][:, :, 1:], time_from_above[0]], 2),
                        jnp.concatenate([apply_ahead_half[1][:, :, 1:], time_from_above[1]], 2),
                    )
                    time_behind_moved = (
                        jnp.concatenate(
                            [time_from_below[0], apply_behind_half[0][:, :, : local_times - 1]], 2
                        ),
                        jnp.concatenate(
                            [time_from_below[1], apply_behind_half[1][:, :, : local_times - 1]], 2
                        ),
                    )
                    apply_ahead_moved = time_ahead_moved
                    apply_behind_moved = time_behind_moved
                else:
                    edge_block = jnp.stack(
                        [
                            jnp.concatenate([apply_ahead_half[0], apply_behind_half[0]], 3),
                            jnp.concatenate([apply_ahead_half[1], apply_behind_half[1]], 3),
                        ]
                    )
                    received = padded(edge_block, (("space", 4),), 1)
                    from_below = received[:, :, :, :, :1] * space_low
                    from_above = received[:, :, :, :, 3:] * space_high
                    ahead_moved = (
                        jnp.concatenate([apply_ahead_half[0][:, :, :, 1:], from_above[0]], 3),
                        jnp.concatenate([apply_ahead_half[1][:, :, :, 1:], from_above[1]], 3),
                    )
                    behind_moved = (
                        jnp.concatenate(
                            [from_below[0], apply_behind_half[0][:, :, :, : local_planes - 1]], 3
                        ),
                        jnp.concatenate(
                            [from_below[1], apply_behind_half[1][:, :, :, : local_planes - 1]], 3
                        ),
                    )
                    apply_ahead_moved = ahead_moved
                    apply_behind_moved = behind_moved
            ahead_linked = link_apply(link_real, link_imag, apply_ahead_moved)
            hopping = pair_add(hopping, recombine(direction, ahead_linked, apply_behind_moved))
        clovered = clover_apply(clover, solution)
        result = pair_add(pair_scale(diag_term, solution), clovered)
        applied = pair_sub(result, pair_scale(0.5, hopping))
        solution = pair_add(solution, pair_scale(step_size, pair_sub(source, applied)))
    partial_sums = project(solution, eigvecs)
    share_rows = partial_sums.shape[0] // lax.axis_size("space")
    summed = lax.psum(partial_sums, "space")
    own_block = lax.dynamic_slice_in_dim(summed, space_rank * share_rows, share_rows, 0)
    weighted = weigh_pairs(own_block, partner)
    correlator = jnp.einsum(
        "jac,jbc->jab",
        weighted,
        lax.all_gather(own_block, "tm", axis=1, tiled=True),
        precision=lax.Precision.HIGHEST,
    )
    return (own_block, correlator)


def solution(mesh):
    return jax.shard_map(
        shards,
        mesh=mesh,
        in_specs=(
            P(None, "tm", "space", None, None),
            P(None, None, "tm", "space", None, None),
            P(None, None, "tm", "space", None, None),
            P(None, "tm", "space", None, None),
            P(),
            P(),
            P(),
        ),
        out_specs=(P("space", "tm", None), P("space", "tm", None)),
        check_vma=False,
    )
```

profile of v0, /device:TPU:0, one launch (start us, length us, event | category | flops | bytes accessed | tf_op | source)
XLA Modules:
  0.0 173.5 jit_solution(8909431335805332813)
XLA Ops:
  0.7 0.8 fusion.418
  2.8 5.1 %collective-permute-start.2 = (f32[2,8,2,1,1,3,256]{6,1,5,2,3,4,0:T(8,128)S(1)}, f32[2,8,2,1,1,3,256]{6,1,5,2,3,4,0:T(8,128)S(1)}, u32[]{:S(2)}, u32[]{:S(2)}) collective-permute-start(f32[2,8,2,1,1,3,256]{6,1,5,2,3,4,0:T(8,128)S(1)} %get-tuple-element.152), channel_id=1, source_target_pairs={{8,0},{16,8},{24,16},{0,24},{9,1},{17,9},{25,17},{1,25},{10,2},{18... | collective-permute-start | bytes 294920 | tf_op jit(solution)/shard_map/ppermute | solution.py:29
  8.1 1.7 collective-permute-start
  10.2 0.8 copy-done.17
  16.5 1.3 add_bitcast_fusion.4
  17.9 1.3 add_bitcast_fusion.17
  25.6 0.9 copy-done
  26.5 0.8 slice_reduce_fusion
  27.4 0.7 fusion.140
  28.1 0.7 fusion.142
  36.3 0.7 fusion.125
  40.4 1.3 add_bitcast_fusion.3
  43.0 1.3 add_bitcast_fusion.12
  47.1 0.7 copy.735
  48.7 2.7 %collective-permute-start.4 = (f32[2,8,2,1,1,3,256]{6,1,5,2,4,3,0:T(8,128)S(1)}, f32[2,8,2,1,1,3,256]{6,1,5,2,4,3,0:T(8,128)S(1)}, u32[]{:S(2)}, u32[]{:S(2)}) collective-permute-start(f32[2,8,2,1,1,3,256]{6,1,5,2,4,3,0:T(8,128)S(1)} %get-tuple-element.150), channel_id=1, source_target_pairs={{1,0},{2,1},{3,2},{4,3},{5,4},{6,5},{7,6},{0,7},{9,8},{10,9},{11,1... | collective-permute-start | bytes 294920 | tf_op jit(solution)/shard_map/ppermute | solution.py:29
  52.2 3.6 %collective-permute-start.6 = (f32[2,8,2,1,1,3,256]{6,1,5,2,3,4,0:T(8,128)S(1)}, f32[2,8,2,1,1,3,256]{6,1,5,2,3,4,0:T(8,128)S(1)}, u32[]{:S(2)}, u32[]{:S(2)}) collective-permute-start(f32[2,8,2,1,1,3,256]{6,1,5,2,3,4,0:T(8,128)S(1)} %get-tuple-element.148), channel_id=1, source_target_pairs={{8,0},{16,8},{24,16},{0,24},{9,1},{17,9},{25,17},{1,25},{10,2},{18... | collective-permute-start | bytes 294920 | tf_op jit(solution)/shard_map/ppermute | solution.py:29
  56.6 0.7 fusion.146
  58.1 0.7 fusion.186
  59.6 0.7 copy-done.81
  61.9 0.7 copy-done.100
  62.6 0.7 copy-done.98
  63.4 0.7 copy-done.96
  78.7 1.3 add_bitcast_fusion
  81.3 1.3 add_bitcast_fusion.8
  85.1 0.7 fusion.123
  87.2 1.4 copy.790
  88.6 1.4 copy.786
  90.0 1.4 copy.787
  91.4 0.7 copy-done.109
  95.3 2.4 %collective-permute-start.8 = (f32[2,8,2,1,1,3,256]{6,1,5,2,4,3,0:T(8,128)S(1)}, f32[2,8,2,1,1,3,256]{6,1,5,2,4,3,0:T(8,128)S(1)}, u32[]{:S(2)}, u32[]{:S(2)}) collective-permute-start(f32[2,8,2,1,1,3,256]{6,1,5,2,4,3,0:T(8,128)S(1)} %get-tuple-element.146), channel_id=1, source_target_pairs={{1,0},{2,1},{3,2},{4,3},{5,4},{6,5},{7,6},{0,7},{9,8},{10,9},{11,1... | collective-permute-start | bytes 294920 | tf_op jit(solution)/shard_map/ppermute | solution.py:29
  98.6 3.8 %collective-permute-start.10 = (f32[2,8,2,1,1,3,256]{6,1,5,2,3,4,0:T(8,128)S(1)}, f32[2,8,2,1,1,3,256]{6,1,5,2,3,4,0:T(8,128)S(1)}, u32[]{:S(2)}, u32[]{:S(2)}) collective-permute-start(f32[2,8,2,1,1,3,256]{6,1,5,2,3,4,0:T(8,128)S(1)} %get-tuple-element.144), channel_id=1, source_target_pairs={{8,0},{16,8},{24,16},{0,24},{9,1},{17,9},{25,17},{1,25},{10,2},{18... | collective-permute-start | bytes 294920 | tf_op jit(solution)/shard_map/ppermute | solution.py:29
  103.2 0.7 fusion.148
  103.9 0.7 fusion.150
  105.5 0.7 copy-done.82
  109.3 0.7 copy-done.92
  110.0 0.7 copy-done.86
  110.8 0.7 copy-done.84
  114.4 0.7 fusion.121
  116.1 0.7 multiply_select_fusion.2
  118.4 0.7 fusion.369
  120.0 2.4 %collective-permute-start.12 = (f32[2,8,2,1,1,3,256]{6,1,5,2,4,3,0:T(8,128)S(1)}, f32[2,8,2,1,1,3,256]{6,1,5,2,4,3,0:T(8,128)S(1)}, u32[]{:S(2)}, u32[]{:S(2)}) collective-permute-start(f32[2,8,2,1,1,3,256]{6,1,5,2,4,3,0:T(8,128)S(1)} %get-tuple-element.142), channel_id=1, source_target_pairs={{1,0},{2,1},{3,2},{4,3},{5,4},{6,5},{7,6},{0,7},{9,8},{10,9},{11,1... | collective-permute-start | bytes 294920 | tf_op jit(solution)/shard_map/ppermute | solution.py:29
  122.5 3.6 %collective-permute-start.14 = (f32[2,8,2,1,1,3,256]{6,1,5,2,3,4,0:T(8,128)S(1)}, f32[2,8,2,1,1,3,256]{6,1,5,2,3,4,0:T(8,128)S(1)}, u32[]{:S(2)}, u32[]{:S(2)}) collective-permute-start(f32[2,8,2,1,1,3,256]{6,1,5,2,3,4,0:T(8,128)S(1)} %get-tuple-element.140), channel_id=1, source_target_pairs={{8,0},{16,8},{24,16},{0,24},{9,1},{17,9},{25,17},{1,25},{10,2},{18... | collective-permute-start | bytes 294920 | tf_op jit(solution)/shard_map/ppermute | solution.py:29
  126.3 1.1 collective-permute-done.13
  127.5 0.8 collective-permute-done.14
  128.4 4.1 %collective-permute-done.15 = f32[2,8,2,1,1,3,256]{6,1,5,2,3,4,0:T(8,128)S(1)} collective-permute-done((f32[2,8,2,1,1,3,256]{6,1,5,2,3,4,0:T(8,128)S(1)}, f32[2,8,2,1,1,3,256]{6,1,5,2,3,4,0:T(8,128)S(1)}, u32[]{:S(2)}, u32[]{:S(2)}) %collective-permute-start.15) | collective-permute-done | bytes 98336 | tf_op jit(solution)/shard_map/ppermute | solution.py:28
  136.2 23.4 %psum.7 = f32[32,1,96]{2,0,1:T(8,128)S(1)} all-reduce(f32[32,1,96]{2,0,1:T(8,128)S(1)} %pad_maximum_fusion.32), channel_id=1, replica_groups=mesh['tm'=4,'space'=8] {'space'}, use_global_device_ids=true, to_apply=%region_0.1 | all-reduce | flops 3072 | bytes 24576 | tf_op jit(solution)/shard_map/psum | solution.py:301
  160.8 11.9 %all_gather.3 = f32[4,4,96]{2,0,1:T(4,128)S(1)} all-gather(f32[4,1,96]{2,0,1:T(4,128)S(1)} %constant_dynamic-slice_fusion), channel_id=1, replica_groups=mesh['tm'=4,'space'=8] {'tm'}, dimensions={1}, use_global_device_ids=true | all-gather | bytes 7680 | tf_op jit(solution)/shard_map/all_gather | solution.py:307
  172.7 0.7 fusion.313
  (828 shorter events, 68.1 us)
Async XLA Ops:
  0.6 0.9 copy-start.113
  1.6 49.8 %copy-start.20 = (f32[1,1,1,3,256]{4,3,2,1,0:T(4,128)}, f32[1,1,1,3,256]{4,3,2,1,0:T(4,128)S(1)}, u32[]{:S(2)}) copy-start(f32[1,1,1,3,256]{4,3,2,1,0:T(4,128)S(1)} %copy.987) | copy-start | bytes 9220
  1.6 49.8 %copy-start.15 = (f32[1,1,1,3,256]{4,3,2,1,0:T(4,128)}, f32[1,1,1,3,256]{4,3,2,1,0:T(4,128)S(1)}, u32[]{:S(2)}) copy-start(f32[1,1,1,3,256]{4,3,2,1,0:T(4,128)S(1)} %copy.983) | copy-start | bytes 9220
  1.7 49.8 %copy-start.22 = (f32[1,1,1,3,256]{4,3,2,1,0:T(4,128)}, f32[1,1,1,3,256]{4,3,2,1,0:T(4,128)S(1)}, u32[]{:S(2)}) copy-start(f32[1,1,1,3,256]{4,3,2,1,0:T(4,128)S(1)} %copy.985) | copy-start | bytes 9220
  2.8 27.8 %collective-permute-start.2 = (f32[2,8,2,1,1,3,256]{6,1,5,2,3,4,0:T(8,128)S(1)}, f32[2,8,2,1,1,3,256]{6,1,5,2,3,4,0:T(8,128)S(1)}, u32[]{:S(2)}, u32[]{:S(2)}) collective-permute-start(f32[2,8,2,1,1,3,256]{6,1,5,2,3,4,0:T(8,128)S(1)} %get-tuple-element.152), channel_id=1, source_target_pairs={{8,0},{16,8},{24,16},{0,24},{9,1},{17,9},{25,17},{1,25},{10,2},{18... | collective-permute-start | bytes 294920 | tf_op jit(solution)/shard_map/ppermute | solution.py:29
  7.9 22.8 %collective-permute-start.3 = (f32[2,8,2,1,1,3,256]{6,1,5,2,3,4,0:T(8,128)S(1)}, f32[2,8,2,1,1,3,256]{6,1,5,2,3,4,0:T(8,128)S(1)}, u32[]{:S(2)}, u32[]{:S(2)}) collective-permute-start(f32[2,8,2,1,1,3,256]{6,1,5,2,3,4,0:T(8,128)S(1)} %get-tuple-element.153), channel_id=1, source_target_pairs={{0,8},{8,16},{16,24},{24,0},{1,9},{9,17},{17,25},{25,1},{2,10},{10... | collective-permute-start | bytes 294920 | tf_op jit(solution)/shard_map/ppermute | solution.py:28
  7.9 40.7 %copy-start.24 = (f32[1,1,1,3,256]{4,3,2,1,0:T(4,128)}, f32[1,1,1,3,256]{4,3,2,1,0:T(4,128)S(1)}, u32[]{:S(2)}) copy-start(f32[1,1,1,3,256]{4,3,2,1,0:T(4,128)S(1)} %copy.998) | copy-start | bytes 9220
  7.9 40.7 %copy-start.26 = (f32[1,1,1,3,256]{4,3,2,1,0:T(4,128)}, f32[1,1,1,3,256]{4,3,2,1,0:T(4,128)S(1)}, u32[]{:S(2)}) copy-start(f32[1,1,1,3,256]{4,3,2,1,0:T(4,128)S(1)} %copy.994) | copy-start | bytes 9220
  7.9 40.7 %copy-start.28 = (f32[1,1,1,3,256]{4,3,2,1,0:T(4,128)}, f32[1,1,1,3,256]{4,3,2,1,0:T(4,128)S(1)}, u32[]{:S(2)}) copy-start(f32[1,1,1,3,256]{4,3,2,1,0:T(4,128)S(1)} %copy.996) | copy-start | bytes 9220
  8.0 40.6 %copy-start.30 = (f32[1,1,1,3,256]{4,3,2,1,0:T(4,128)}, f32[1,1,1,3,256]{4,3,2,1,0:T(4,128)S(1)}, u32[]{:S(2)}) copy-start(f32[1,1,1,3,256]{4,3,2,1,0:T(4,128)S(1)} %copy.999) | copy-start | bytes 9220
  8.0 40.6 %copy-start.32 = (f32[1,1,1,3,256]{4,3,2,1,0:T(4,128)}, f32[1,1,1,3,256]{4,3,2,1,0:T(4,128)S(1)}, u32[]{:S(2)}) copy-start(f32[1,1,1,3,256]{4,3,2,1,0:T(4,128)S(1)} %copy.995) | copy-start | bytes 9220
  8.0 40.6 %copy-start.34 = (f32[1,1,1,3,256]{4,3,2,1,0:T(4,128)}, f32[1,1,1,3,256]{4,3,2,1,0:T(4,128)S(1)}, u32[]{:S(2)}) copy-start(f32[1,1,1,3,256]{4,3,2,1,0:T(4,128)S(1)} %copy.997) | copy-start | bytes 9220
  8.1 22.2 %collective-permute-start = (f32[2,8,2,1,1,3,256]{6,1,5,2,4,3,0:T(8,128)S(1)}, f32[2,8,2,1,1,3,256]{6,1,5,2,4,3,0:T(8,128)S(1)}, u32[]{:S(2)}, u32[]{:S(2)}) collective-permute-start(f32[2,8,2,1,1,3,256]{6,1,5,2,4,3,0:T(8,128)S(1)} %get-tuple-element.154), channel_id=1, source_target_pairs={{1,0},{2,1},{3,2},{4,3},{5,4},{6,5},{7,6},{0,7},{9,8},{10,9},{11,1... | collective-permute-start | bytes 294920 | tf_op jit(solution)/shard_map/ppermute | solution.py:29
  9.8 20.7 %collective-permute-start.1 = (f32[2,8,2,1,1,3,256]{6,1,5,2,4,3,0:T(8,128)S(1)}, f32[2,8,2,1,1,3,256]{6,1,5,2,4,3,0:T(8,128)S(1)}, u32[]{:S(2)}, u32[]{:S(2)}) collective-permute-start(f32[2,8,2,1,1,3,256]{6,1,5,2,4,3,0:T(8,128)S(1)} %get-tuple-element.155), channel_id=1, source_target_pairs={{0,1},{1,2},{2,3},{3,4},{4,5},{5,6},{6,7},{7,0},{8,9},{9,10},{10,1... | collective-permute-start | bytes 294920 | tf_op jit(solution)/shard_map/ppermute | solution.py:28
  10.1 0.9 copy-start.17
  12.6 26.8 %copy-start.36 = (f32[1,1,1,3,256]{4,3,2,1,0:T(4,128)}, f32[1,1,1,3,256]{4,3,2,1,0:T(4,128)S(1)}, u32[]{:S(2)}) copy-start(f32[1,1,1,3,256]{4,3,2,1,0:T(4,128)S(1)} %copy.1006) | copy-start | bytes 9220
  12.6 26.8 %copy-start.39 = (f32[1,1,1,3,256]{4,3,2,1,0:T(4,128)}, f32[1,1,1,3,256]{4,3,2,1,0:T(4,128)S(1)}, u32[]{:S(2)}) copy-start(f32[1,1,1,3,256]{4,3,2,1,0:T(4,128)S(1)} %copy.1002) | copy-start | bytes 9220
  12.6 26.8 %copy-start.42 = (f32[1,1,1,3,256]{4,3,2,1,0:T(4,128)}, f32[1,1,1,3,256]{4,3,2,1,0:T(4,128)S(1)}, u32[]{:S(2)}) copy-start(f32[1,1,1,3,256]{4,3,2,1,0:T(4,128)S(1)} %copy.1004) | copy-start | bytes 9220
  12.6 26.8 %copy-start.45 = (f32[1,1,1,3,256]{4,3,2,1,0:T(4,128)}, f32[1,1,1,3,256]{4,3,2,1,0:T(4,128)S(1)}, u32[]{:S(2)}) copy-start(f32[1,1,1,3,256]{4,3,2,1,0:T(4,128)S(1)} %copy.1005) | copy-start | bytes 9220
  12.6 26.8 %copy-start.48 = (f32[1,1,1,3,256]{4,3,2,1,0:T(4,128)}, f32[1,1,1,3,256]{4,3,2,1,0:T(4,128)S(1)}, u32[]{:S(2)}) copy-start(f32[1,1,1,3,256]{4,3,2,1,0:T(4,128)S(1)} %copy.1001) | copy-start | bytes 9220
  12.7 26.8 %copy-start.51 = (f32[1,1,1,3,256]{4,3,2,1,0:T(4,128)}, f32[1,1,1,3,256]{4,3,2,1,0:T(4,128)S(1)}, u32[]{:S(2)}) copy-start(f32[1,1,1,3,256]{4,3,2,1,0:T(4,128)S(1)} %copy.1003) | copy-start | bytes 9220
  13.3 21.5 %copy-start.54 = (f32[1,1,1,3,256]{4,3,2,1,0:T(4,128)}, f32[1,1,1,3,256]{4,3,2,1,0:T(4,128)S(1)}, u32[]{:S(2)}) copy-start(f32[1,1,1,3,256]{4,3,2,1,0:T(4,128)S(1)} %copy.1017) | copy-start | bytes 9220
  13.3 21.5 %copy-start.57 = (f32[1,1,1,3,256]{4,3,2,1,0:T(4,128)}, f32[1,1,1,3,256]{4,3,2,1,0:T(4,128)S(1)}, u32[]{:S(2)}) copy-start(f32[1,1,1,3,256]{4,3,2,1,0:T(4,128)S(1)} %copy.1013) | copy-start | bytes 9220
  13.3 21.5 %copy-start.60 = (f32[1,1,1,3,256]{4,3,2,1,0:T(4,128)}, f32[1,1,1,3,256]{4,3,2,1,0:T(4,128)S(1)}, u32[]{:S(2)}) copy-start(f32[1,1,1,3,256]{4,3,2,1,0:T(4,128)S(1)} %copy.1015) | copy-start | bytes 9220
  13.3 21.5 %copy-start.63 = (f32[1,1,1,3,256]{4,3,2,1,0:T(4,128)}, f32[1,1,1,3,256]{4,3,2,1,0:T(4,128)S(1)}, u32[]{:S(2)}) copy-start(f32[1,1,1,3,256]{4,3,2,1,0:T(4,128)S(1)} %copy.1018) | copy-start | bytes 9220
  13.3 21.4 %copy-start.66 = (f32[1,1,1,3,256]{4,3,2,1,0:T(4,128)}, f32[1,1,1,3,256]{4,3,2,1,0:T(4,128)S(1)}, u32[]{:S(2)}) copy-start(f32[1,1,1,3,256]{4,3,2,1,0:T(4,128)S(1)} %copy.1014) | copy-start | bytes 9220
  13.4 21.4 %copy-start.69 = (f32[1,1,1,3,256]{4,3,2,1,0:T(4,128)}, f32[1,1,1,3,256]{4,3,2,1,0:T(4,128)S(1)}, u32[]{:S(2)}) copy-start(f32[1,1,1,3,256]{4,3,2,1,0:T(4,128)S(1)} %copy.1016) | copy-start | bytes 9220
  25.5 1.0 copy-start
  48.7 15.4 %collective-permute-start.4 = (f32[2,8,2,1,1,3,256]{6,1,5,2,4,3,0:T(8,128)S(1)}, f32[2,8,2,1,1,3,256]{6,1,5,2,4,3,0:T(8,128)S(1)}, u32[]{:S(2)}, u32[]{:S(2)}) collective-permute-start(f32[2,8,2,1,1,3,256]{6,1,5,2,4,3,0:T(8,128)S(1)} %get-tuple-element.150), channel_id=1, source_target_pairs={{1,0},{2,1},{3,2},{4,3},{5,4},{6,5},{7,6},{0,7},{9,8},{10,9},{11,1... | collective-permute-start | bytes 294920 | tf_op jit(solution)/shard_map/ppermute | solution.py:29
  51.4 12.8 %collective-permute-start.5 = (f32[2,8,2,1,1,3,256]{6,1,5,2,4,3,0:T(8,128)S(1)}, f32[2,8,2,1,1,3,256]{6,1,5,2,4,3,0:T(8,128)S(1)}, u32[]{:S(2)}, u32[]{:S(2)}) collective-permute-start(f32[2,8,2,1,1,3,256]{6,1,5,2,4,3,0:T(8,128)S(1)} %get-tuple-element.151), channel_id=1, source_target_pairs={{0,1},{1,2},{2,3},{3,4},{4,5},{5,6},{6,7},{7,0},{8,9},{9,10},{10,1... | collective-permute-start | bytes 294920 | tf_op jit(solution)/shard_map/ppermute | solution.py:28
  52.2 12.7 %collective-permute-start.6 = (f32[2,8,2,1,1,3,256]{6,1,5,2,3,4,0:T(8,128)S(1)}, f32[2,8,2,1,1,3,256]{6,1,5,2,3,4,0:T(8,128)S(1)}, u32[]{:S(2)}, u32[]{:S(2)}) collective-permute-start(f32[2,8,2,1,1,3,256]{6,1,5,2,3,4,0:T(8,128)S(1)} %get-tuple-element.148), channel_id=1, source_target_pairs={{8,0},{16,8},{24,16},{0,24},{9,1},{17,9},{25,17},{1,25},{10,2},{18... | collective-permute-start | bytes 294920 | tf_op jit(solution)/shard_map/ppermute | solution.py:29
  55.8 9.8 %collective-permute-start.7 = (f32[2,8,2,1,1,3,256]{6,1,5,2,3,4,0:T(8,128)S(1)}, f32[2,8,2,1,1,3,256]{6,1,5,2,3,4,0:T(8,128)S(1)}, u32[]{:S(2)}, u32[]{:S(2)}) collective-permute-start(f32[2,8,2,1,1,3,256]{6,1,5,2,3,4,0:T(8,128)S(1)} %get-tuple-element.149), channel_id=1, source_target_pairs={{0,8},{8,16},{16,24},{24,0},{1,9},{9,17},{17,25},{25,1},{2,10},{10... | collective-permute-start | bytes 294920 | tf_op jit(solution)/shard_map/ppermute | solution.py:28
  95.3 16.2 %collective-permute-start.8 = (f32[2,8,2,1,1,3,256]{6,1,5,2,4,3,0:T(8,128)S(1)}, f32[2,8,2,1,1,3,256]{6,1,5,2,4,3,0:T(8,128)S(1)}, u32[]{:S(2)}, u32[]{:S(2)}) collective-permute-start(f32[2,8,2,1,1,3,256]{6,1,5,2,4,3,0:T(8,128)S(1)} %get-tuple-element.146), channel_id=1, source_target_pairs={{1,0},{2,1},{3,2},{4,3},{5,4},{6,5},{7,6},{0,7},{9,8},{10,9},{11,1... | collective-permute-start | bytes 294920 | tf_op jit(solution)/shard_map/ppermute | solution.py:29
  97.8 13.8 %collective-permute-start.9 = (f32[2,8,2,1,1,3,256]{6,1,5,2,4,3,0:T(8,128)S(1)}, f32[2,8,2,1,1,3,256]{6,1,5,2,4,3,0:T(8,128)S(1)}, u32[]{:S(2)}, u32[]{:S(2)}) collective-permute-start(f32[2,8,2,1,1,3,256]{6,1,5,2,4,3,0:T(8,128)S(1)} %get-tuple-element.147), channel_id=1, source_target_pairs={{0,1},{1,2},{2,3},{3,4},{4,5},{5,6},{6,7},{7,0},{8,9},{9,10},{10,1... | collective-permute-start | bytes 294920 | tf_op jit(solution)/shard_map/ppermute | solution.py:28
  98.6 13.1 %collective-permute-start.10 = (f32[2,8,2,1,1,3,256]{6,1,5,2,3,4,0:T(8,128)S(1)}, f32[2,8,2,1,1,3,256]{6,1,5,2,3,4,0:T(8,128)S(1)}, u32[]{:S(2)}, u32[]{:S(2)}) collective-permute-start(f32[2,8,2,1,1,3,256]{6,1,5,2,3,4,0:T(8,128)S(1)} %get-tuple-element.144), channel_id=1, source_target_pairs={{8,0},{16,8},{24,16},{0,24},{9,1},{17,9},{25,17},{1,25},{10,2},{18... | collective-permute-start | bytes 294920 | tf_op jit(solution)/shard_map/ppermute | solution.py:29
  102.4 9.4 %collective-permute-start.11 = (f32[2,8,2,1,1,3,256]{6,1,5,2,3,4,0:T(8,128)S(1)}, f32[2,8,2,1,1,3,256]{6,1,5,2,3,4,0:T(8,128)S(1)}, u32[]{:S(2)}, u32[]{:S(2)}) collective-permute-start(f32[2,8,2,1,1,3,256]{6,1,5,2,3,4,0:T(8,128)S(1)} %get-tuple-element.145), channel_id=1, source_target_pairs={{0,8},{8,16},{16,24},{24,0},{1,9},{9,17},{17,25},{25,1},{2,10},{10... | collective-permute-start | bytes 294920 | tf_op jit(solution)/shard_map/ppermute | solution.py:28
  120.0 6.2 %collective-permute-start.12 = (f32[2,8,2,1,1,3,256]{6,1,5,2,4,3,0:T(8,128)S(1)}, f32[2,8,2,1,1,3,256]{6,1,5,2,4,3,0:T(8,128)S(1)}, u32[]{:S(2)}, u32[]{:S(2)}) collective-permute-start(f32[2,8,2,1,1,3,256]{6,1,5,2,4,3,0:T(8,128)S(1)} %get-tuple-element.142), channel_id=1, source_target_pairs={{1,0},{2,1},{3,2},{4,3},{5,4},{6,5},{7,6},{0,7},{9,8},{10,9},{11,1... | collective-permute-start | bytes 294920 | tf_op jit(solution)/shard_map/ppermute | solution.py:29
  122.4 4.9 %collective-permute-start.13 = (f32[2,8,2,1,1,3,256]{6,1,5,2,4,3,0:T(8,128)S(1)}, f32[2,8,2,1,1,3,256]{6,1,5,2,4,3,0:T(8,128)S(1)}, u32[]{:S(2)}, u32[]{:S(2)}) collective-permute-start(f32[2,8,2,1,1,3,256]{6,1,5,2,4,3,0:T(8,128)S(1)} %get-tuple-element.143), channel_id=1, source_target_pairs={{0,1},{1,2},{2,3},{3,4},{4,5},{5,6},{6,7},{7,0},{8,9},{9,10},{10,1... | collective-permute-start | bytes 294920 | tf_op jit(solution)/shard_map/ppermute | solution.py:28
  122.5 5.8 %collective-permute-start.14 = (f32[2,8,2,1,1,3,256]{6,1,5,2,3,4,0:T(8,128)S(1)}, f32[2,8,2,1,1,3,256]{6,1,5,2,3,4,0:T(8,128)S(1)}, u32[]{:S(2)}, u32[]{:S(2)}) collective-permute-start(f32[2,8,2,1,1,3,256]{6,1,5,2,3,4,0:T(8,128)S(1)} %get-tuple-element.140), channel_id=1, source_target_pairs={{8,0},{16,8},{24,16},{0,24},{9,1},{17,9},{25,17},{1,25},{10,2},{18... | collective-permute-start | bytes 294920 | tf_op jit(solution)/shard_map/ppermute | solution.py:29
  126.1 6.4 %collective-permute-start.15 = (f32[2,8,2,1,1,3,256]{6,1,5,2,3,4,0:T(8,128)S(1)}, f32[2,8,2,1,1,3,256]{6,1,5,2,3,4,0:T(8,128)S(1)}, u32[]{:S(2)}, u32[]{:S(2)}) collective-permute-start(f32[2,8,2,1,1,3,256]{6,1,5,2,3,4,0:T(8,128)S(1)} %get-tuple-element.141), channel_id=1, source_target_pairs={{0,8},{8,16},{16,24},{24,0},{1,9},{9,17},{17,25},{25,1},{2,10},{10... | collective-permute-start | bytes 294920 | tf_op jit(solution)/shard_map/ppermute | solution.py:28
  132.6 0.8 copy-start.8
  132.6 0.9 copy-start.11
  132.6 0.9 copy-start.12
  132.6 0.9 copy-start.14
  133.8 0.8 copy-start.13
  133.9 0.8 copy-start.1
  133.9 0.9 copy-start.3
  133.9 0.9 copy-start.4
  (94 other events, 68.2 us)
where the time goes:
time: 176 us; the launch traced here: 173 us
  local copies, waits for them, and re-layouts  49.1 us (28%)
  other arithmetic  48.4 us (28%)
  blocking collectives  35.2 us (20%)
  starting transfers between devices  25.2 us (14%)
  between operations  7.38 us (4%)
  waiting for transfers between devices  6.06 us (3%)
  matrix products  2.15 us (1%)
    ppermute x8, starting transfers between devices, padded(): after = lax.ppermute(initial, axis, down)  25.2 us
    psum x1, blocking collectives, shards(): summed = lax.psum(partial_sums, 'space')  23.4 us
    unnamed x304, local copies, waits for them, and re-layouts  23.2 us
    add x41, other arithmetic, pair_add(): return (first_pair[0] + second_pair[0], first_pair[1] + second_pair[1])  16.8 us
    all_gather x1, blocking collectives, shards(): lax.all_gather(own_block, 'tm', axis=1, tiled=True)  11.9 us
    ppermute x8, waiting for transfers between devices, padded(): before = lax.ppermute(last, axis, up)  5.22 us
    concatenate x21, other arithmetic, recombine(): jnp.concatenate([top_part[0], bottom_part[0]], 1)  4.73 us
    concatenate x9, local copies, waits for them, and re-layouts, plane_shift(): jnp.roll(values, 1, axis=-1)  4.47 us
  transfers between devices with their start and end apart: 16, of which 3 were waited for; matrix products, arithmetic and copies ran while one was open for 13% of the time, Pallas kernels for 0%

commit v1 on v0

v1 whole, which is shorter than its diff:
```python
import functools
import math

import jax
import jax.numpy as jnp
from jax import lax
from jax.experimental import pallas as pl
from jax.experimental.pallas import tpu as pltpu
from jax.sharding import PartitionSpec as P

ITERS = 4
DILUTE = 4
MESH = pl.DeviceIdType.MESH

diag_term = 4.1
step_size = 0.2
twist_table = (
    (((1, 0, -1), (0, 0, -1)), ((1, 0, 1), (0, 0, 1))),
    (((1, -1, 0), (0, 1, 0)), ((1, 1, 0), (0, -1, 0))),
    (((0, 0, -1), (1, 0, 1)), ((0, 0, 1), (1, 0, -1))),
    (((0, 1, 0), (1, 1, 0)), ((0, 1, 0), (1, 1, 0))),
)


def signed_add(total, sign, value):
    return total + value if sign > 0 else total - value


def twist_terms(real_coef, imag_coef, real, imag):
    if imag_coef == 0:
        return (real_coef, real), (real_coef, imag)
    return (-imag_coef, imag), (imag_coef, real)


def kernel(
    times, planes, noise, gauge, clover, eigvecs, partner, dilution, boundary,
    per_out, cor_out,
    links, clov, src, sol, acc, sbuf, rbuf, eig_hi, eig_lo, part, red, own, gat, onehot,
    ssem, rsem, red_ssem, red_rsem, gat_ssem, gat_rsem,
):
    t_me = lax.axis_index("tm")
    z_me = lax.axis_index("space")
    t_up, t_down = lax.rem(t_me + 1, times), lax.rem(t_me + times - 1, times)
    z_up, z_down = lax.rem(z_me + 1, planes), lax.rem(z_me + planes - 1, planes)

    barrier = pltpu.get_barrier_semaphore()
    for off in range(1, times):
        pl.semaphore_signal(
            barrier, inc=1, device_id={"tm": lax.rem(t_me + off, times)}, device_id_type=MESH
        )
    for off in range(1, planes):
        pl.semaphore_signal(
            barrier, inc=1, device_id={"space": lax.rem(z_me + off, planes)}, device_id_type=MESH
        )

    nsrc, sites = noise.shape[0], noise.shape[-1]
    side = math.isqrt(sites)
    nev = eigvecs.shape[0]
    row = (1, sites)
    lane = lax.broadcasted_iota(jnp.int32, row, 1)
    x_row, y_row = lax.rem(lane, side), lax.div(lane, side)
    phases = [1.0 - 2.0 * boundary[mu].astype(jnp.float32) for mu in range(4)]
    half_step = 0.5 * step_size
    one = jnp.ones(row, jnp.float32)
    signs = (
        jnp.where(x_row == side - 1, phases[0], one) * half_step,
        jnp.where(y_row == side - 1, phases[1], one) * half_step,
        jnp.where(z_me == planes - 1, phases[2], 1.0) * half_step * one,
        jnp.where(t_me == times - 1, phases[3], 1.0) * half_step * one,
    )
    for mu in range(4):
        for col in range(3):
            for p in range(2):
                k = 2 * col + p
                value = gauge[mu, :, 0, 0, k : k + 1, :] * signs[mu][None]
                links[mu, p, :, col] = jnp.broadcast_to(value, (3, nsrc, sites))

    field = (nsrc, sites)
    source_row = lax.broadcasted_iota(jnp.int32, field, 0)
    spin_row = lax.rem(source_row, 4)
    t_mod = lax.rem(t_me, DILUTE)
    weight = jnp.zeros(field, jnp.float32)
    for j in range(nsrc):
        chosen = jnp.where(dilution[j] == t_mod, step_size, 0.0)
        weight = jnp.where(source_row == j, chosen, weight)
    for color in range(3):
        for p in range(2):
            value = noise[:, 0, 0, 2 * color + p, :] * weight
            for s in range(4):
                src[p, s, color] = jnp.where(spin_row == s, value, 0.0)
    sol[...] = src[...]

    for b in range(6):
        for p in range(2):
            k = 2 * b + p
            value = clover[:, :, 0, 0, k : k + 1, :] * (-step_size)
            clov[:, p, :, b] = jnp.broadcast_to(value, (2, 6, nsrc, sites))

    for color in range(3):
        real = eigvecs[:, 0, 0, 2 * color, :]
        imag = eigvecs[:, 0, 0, 2 * color + 1, :]
        for p, (top, bottom) in enumerate(((real, -imag), (imag, real))):
            lo = (2 * color + p) * sites
            whole = jnp.concatenate([top, bottom], 0)
            high = whole.astype(jnp.bfloat16)
            eig_hi[:, lo : lo + sites] = high
            eig_lo[:, lo : lo + sites] = (whole - high.astype(jnp.float32)).astype(jnp.bfloat16)

    out_lane = lax.broadcasted_iota(jnp.int32, (1, onehot.shape[1]), 1)
    for k in range(nev):
        for p in range(2):
            onehot[p * nev + k : p * nev + k + 1, :] = jnp.where(
                out_lane == partner[k] + p * nev, 1.0, 0.0
            )

    def half(mu, sign):
        real, imag = [], []
        for h in range(2):
            pick, rc, ic = twist_table[mu][0][h]
            tr, ti = twist_terms(rc, ic, sol[0, 2 + pick], sol[1, 2 + pick])
            real.append(signed_add(sol[0, h], sign * tr[0], tr[1]))
            imag.append(signed_add(sol[1, h], sign * ti[0], ti[1]))
        return jnp.stack(real), jnp.stack(imag)

    def forward(mu, vr, vi):
        real = imag = None
        for c in range(3):
            ur, ui = links[mu, 0, :, c][None], links[mu, 1, :, c][None]
            ar, ai = vr[:, c : c + 1], vi[:, c : c + 1]
            dr, di = ur * ar - ui * ai, ur * ai + ui * ar
            real, imag = (dr, di) if c == 0 else (real + dr, imag + di)
        return real, imag

    def adjoint(mu, vr, vi):
        real = imag = None
        for c in range(3):
            ur, ui = links[mu, 0, c][None], links[mu, 1, c][None]
            ar, ai = vr[:, c : c + 1], vi[:, c : c + 1]
            dr, di = ur * ar + ui * ai, ur * ai - ui * ar
            real, imag = (dr, di) if c == 0 else (real + dr, imag + di)
        return real, imag

    def gather_in(mu, ahead, behind):
        diff = (behind[0] - ahead[0], behind[1] - ahead[1])
        for p in range(2):
            acc[p, 0:2] += ahead[p] + behind[p]
        for h in range(2):
            pick, rc, ic = twist_table[mu][1][h]
            terms = twist_terms(rc, ic, diff[0][pick], diff[1][pick])
            for p in range(2):
                acc[p, 2 + h] = signed_add(acc[p, 2 + h], terms[p][0], terms[p][1])

    flat = (6 * nsrc, sites)
    flat_x = lax.rem(lax.broadcasted_iota(jnp.int32, flat, 1), side)

    def shift(mu, ahead, value):
        value = value.reshape(flat)
        if mu == 0:
            if ahead:
                moved = jnp.where(
                    flat_x == side - 1,
                    pltpu.roll(value, side - 1, 1),
                    pltpu.roll(value, sites - 1, 1),
                )
            else:
                moved = jnp.where(
                    flat_x == 0,
                    pltpu.roll(value, sites - side + 1, 1),
                    pltpu.roll(value, 1, 1),
                )
        else:
            moved = pltpu.roll(value, sites - side if ahead else side, 1)
        return moved.reshape(2, 3, nsrc, sites)

    targets = ({"tm": t_down}, {"tm": t_up}, {"space": z_down}, {"space": z_up})

    def copy(it, d):
        return pltpu.make_async_remote_copy(
            src_ref=sbuf.at[it, d],
            dst_ref=rbuf.at[it, d],
            send_sem=ssem.at[it, d],
            recv_sem=rsem.at[it, d],
            device_id=targets[d],
            device_id_type=MESH,
        )

    pl.semaphore_wait(barrier, times + planes - 2)

    def iteration(it, carry):
        for mu, d in ((3, 0), (2, 2)):
            ahead = half(mu, -1)
            sbuf[it, d, 0], sbuf[it, d, 1] = ahead
            copy(it, d).start()
            behind = adjoint(mu, *half(mu, 1))
            sbuf[it, d + 1, 0], sbuf[it, d + 1, 1] = behind
            copy(it, d + 1).start()
        keep = 1.0 - step_size * diag_term
        for h in range(2):
            real = imag = None
            for b in range(6):
                cr, ci = clov[h, 0, :, b], clov[h, 1, :, b]
                vr = sol[0, 2 * h + b // 3, b % 3][None]
                vi = sol[1, 2 * h + b // 3, b % 3][None]
                dr, di = cr * vr - ci * vi, cr * vi + ci * vr
                real, imag = (dr, di) if b == 0 else (real + dr, imag + di)
            for p, value in enumerate((real, imag)):
                lo = 2 * h
                acc[p, lo : lo + 2] = (
                    value.reshape(2, 3, nsrc, sites)
                    + keep * sol[p, lo : lo + 2]
                    + src[p, lo : lo + 2]
                )
        for mu in range(2):
            ahead = half(mu, -1)
            ahead = forward(mu, shift(mu, True, ahead[0]), shift(mu, True, ahead[1]))
            behind = adjoint(mu, *half(mu, 1))
            behind = (shift(mu, False, behind[0]), shift(mu, False, behind[1]))
            gather_in(mu, ahead, behind)
        for mu, d in ((2, 2), (3, 0)):
            copy(it, d).wait()
            copy(it, d + 1).wait()
            ahead = forward(mu, rbuf[it, d, 0], rbuf[it, d, 1])
            gather_in(mu, ahead, (rbuf[it, d + 1, 0], rbuf[it, d + 1, 1]))
        sol[...] = acc[...]
        return carry

    lax.fori_loop(0, ITERS, iteration, 0)

    pieces = []
    for color in range(3):
        for p in range(2):
            pieces.append(sol[p, :, color].reshape(4 * nsrc, sites))
    whole = jnp.concatenate(pieces, 1)
    high = whole.astype(jnp.bfloat16)
    low = (whole - high.astype(jnp.float32)).astype(jnp.bfloat16)
    dims = (((1,), (1,)), ((), ()))
    eh, el = eig_hi[...], eig_lo[...]
    sums = lax.dot_general(high, eh, dims, preferred_element_type=jnp.float32)
    sums += lax.dot_general(high, el, dims, preferred_element_type=jnp.float32)
    sums += lax.dot_general(low, eh, dims, preferred_element_type=jnp.float32)
    for s in range(4):
        for j in range(nsrc):
            part[4 * j + s] = sums[nsrc * s + j : nsrc * s + j + 1, :]

    share = own.shape[0]

    def reduce_copy(off):
        dst = lax.rem(z_me + off, planes)
        return pltpu.make_async_remote_copy(
            src_ref=part.at[pl.ds(dst * share, share)],
            dst_ref=red.at[off - 1],
            send_sem=red_ssem.at[off - 1],
            recv_sem=red_rsem.at[off - 1],
            device_id={"space": dst},
            device_id_type=MESH,
        )

    def gather_copy(off):
        return pltpu.make_async_remote_copy(
            src_ref=own,
            dst_ref=gat.at[off - 1],
            send_sem=gat_ssem.at[off - 1],
            recv_sem=gat_rsem.at[off - 1],
            device_id={"tm": lax.rem(t_me + off, times)},
            device_id_type=MESH,
        )

    for off in range(1, planes):
        reduce_copy(off).start()
    total = part[pl.ds(z_me * share, share)]
    for off in range(1, planes):
        reduce_copy(off).wait_recv()
        total = total + red[off - 1]
    own[...] = total
    for off in range(1, times):
        gather_copy(off).start()
    per_out[...] = total
    weighted = jnp.dot(
        total.reshape(share, 2 * nev),
        onehot[...],
        preferred_element_type=jnp.float32,
        precision=lax.Precision.HIGHEST,
    ).reshape(share, 1, 2 * nev)
    slot = lax.broadcasted_iota(jnp.int32, (share, 1, times), 2)
    value = jnp.sum(weighted * total, axis=-1, keepdims=True)
    result = jnp.where(slot == t_me, value, 0.0)
    for off in range(1, times):
        gather_copy(off).wait_recv()
        value = jnp.sum(weighted * gat[off - 1], axis=-1, keepdims=True)
        result = jnp.where(slot == lax.rem(t_me + times - off, times), value, result)
    cor_out[...] = result
    for off in range(1, planes):
        reduce_copy(off).wait_send()
    for off in range(1, times):
        gather_copy(off).wait_send()


def shards(times, planes, *args):
    noise, gauge, clover, eigvecs = args[:4]
    assert noise.shape[1] == noise.shape[2] == 1
    nsrc, sites, nev = noise.shape[0], noise.shape[-1], eigvecs.shape[0]
    rows = 4 * nsrc
    share = rows // planes
    depth = 6 * sites
    f32 = jnp.float32
    vmem = pl.BlockSpec(memory_space=pltpu.VMEM)
    smem = pl.BlockSpec(memory_space=pltpu.SMEM)
    dma = pltpu.SemaphoreType.DMA
    return pl.pallas_call(
        functools.partial(kernel, times, planes),
        out_shape=(
            jax.ShapeDtypeStruct((share, 1, 2 * nev), f32),
            jax.ShapeDtypeStruct((share, 1, times), f32),
        ),
        in_specs=[vmem] * 4 + [smem] * 3,
        out_specs=(vmem, vmem),
        scratch_shapes=[
            pltpu.VMEM((4, 2, 3, 3, nsrc, sites), f32),
            pltpu.VMEM((2, 2, 6, 6, nsrc, sites), f32),
            pltpu.VMEM((2, 4, 3, nsrc, sites), f32),
            pltpu.VMEM((2, 4, 3, nsrc, sites), f32),
            pltpu.VMEM((2, 4, 3, nsrc, sites), f32),
            pltpu.VMEM((ITERS, 4, 2, 2, 3, nsrc, sites), f32),
            pltpu.VMEM((ITERS, 4, 2, 2, 3, nsrc, sites), f32),
            pltpu.VMEM((2 * nev, depth), jnp.bfloat16),
            pltpu.VMEM((2 * nev, depth), jnp.bfloat16),
            pltpu.VMEM((rows, 1, 2 * nev), f32),
            pltpu.VMEM((planes - 1, share, 1, 2 * nev), f32),
            pltpu.VMEM((share, 1, 2 * nev), f32),
            pltpu.VMEM((times - 1, share, 1, 2 * nev), f32),
            pltpu.VMEM((2 * nev, 2 * nev), f32),
            dma((ITERS, 4)),
            dma((ITERS, 4)),
            dma((planes - 1,)),
            dma((planes - 1,)),
            dma((times - 1,)),
            dma((times - 1,)),
        ],
        compiler_params=pltpu.CompilerParams(
            collective_id=0, has_side_effects=True, vmem_limit_bytes=32 * 1024 * 1024
        ),
    )(*args)


def solution(mesh):
    return jax.shard_map(
        functools.partial(shards, mesh.shape["tm"], mesh.shape["space"]),
        mesh=mesh,
        in_specs=(
            P(None, "tm", "space", None, None),
            P(None, None, "tm", "space", None, None),
            P(None, None, "tm", "space", None, None),
            P(None, "tm", "space", None, None),
            P(),
            P(),
            P(),
        ),
        out_specs=(P("space", "tm", None), P("space", "tm", None)),
        check_vma=False,
    )
```

time: 176 us -> 42.4 us (0.24); the launches traced: 173 us -> 42.2 us
  other arithmetic: 48.4 us -> 0 us
  local copies, waits for them, and re-layouts: 49.1 us -> 4.5 us
  Pallas kernels: 0 us -> 37 us
  blocking collectives: 35.2 us -> 0 us
  starting transfers between devices: 25.2 us -> 0 us
  between operations: 7.38 us -> 0.69 us
  waiting for transfers between devices: 6.06 us -> 0 us
  matrix products: 2.15 us -> 0 us
    pallas_call x0 -> x1, Pallas kernels: none -> 37 us  [shards(): pl.pallas_call(functools.partial(kernel, times, planes), out_shape=(jax.S...]
    ppermute x16 -> x0, starting transfers between devices: 25.2 us -> none  [the longest x8 25.2 us: padded(): after = lax.ppermute(initial, axis, down)]
    psum x1 -> x0, blocking collectives: 23.4 us -> none  [shards(): summed = lax.psum(partial_sums, 'space')]
    add x61 -> x0, other arithmetic: 20.3 us -> none  [the longest x41 16.8 us: pair_add(): return (first_pair[0] + second_pair[0], first_pair[1] + second_pair[1])]
    unnamed x304 -> x14, local copies, waits for them, and re-layouts: 23.2 us -> 4.5 us
    slice x119 -> x0, local copies, waits for them, and re-layouts: 14.7 us -> none  [the longest x24 4.43 us: spin_twist(): picked = (half_pair[0][:, source_spin], half_pair[1][:, source_spin])]
    all_gather x1 -> x0, blocking collectives: 11.9 us -> none  [shards(): lax.all_gather(own_block, 'tm', axis=1, tiled=True)]
    concatenate x50 -> x0, other arithmetic: 10.1 us -> none  [the longest x21 4.73 us: recombine(): jnp.concatenate([top_part[0], bottom_part[0]], 1)]
  transfers between devices with their start and end apart: 16 -> 0, of which waited for: 3 -> 0; matrix products, arithmetic and copies ran while one was open for 13% -> 0% of each run, Pallas kernels for 0% -> 0%
where the time goes in v1:
time: 42.4 us; the launch traced here: 42.2 us
  Pallas kernels  37 us (87%)
  local copies, waits for them, and re-layouts  4.5 us (11%)
  between operations  0.69 us (2%)
    pallas_call x1, Pallas kernels, shards(): pl.pallas_call(functools.partial(kernel, times, planes), out_shape=(jax.S...  37 us
    unnamed x14, local copies, waits for them, and re-layouts  4.5 us

profile of v1, /device:TPU:0, one launch (start us, length us, event | category | flops | bytes accessed | tf_op | source)
XLA Modules:
  0.0 42.2 jit_solution(14810715767315193818)
XLA Ops:
  0.6 0.0 copy-start.3
  0.6 0.9 %copy.9.noise = f32[8,1,1,6,256]{4,3,2,1,0:T(8,128)S(1)} copy(f32[8,1,1,6,256]{4,2,3,1,0:T(1,128)} %param.7) | data formatting | bytes 98304 | tf_op args[0]
  1.5 0.9 %copy.10.gauge = f32[4,3,1,1,6,256]{5,4,3,2,1,0:T(8,128)S(1)} copy(f32[4,3,1,1,6,256]{5,3,4,2,1,0:T(1,128)} %param.8) | data formatting | bytes 147456 | tf_op args[1]
  2.4 0.9 %copy.11.clover = f32[2,6,1,1,12,256]{5,4,3,2,1,0:T(8,128)S(1)} copy(f32[2,6,1,1,12,256]{5,3,4,2,1,0:T(1,128)} %param.9) | data formatting | bytes 294912 | tf_op args[2]
  3.3 0.0 copy-done.3
  3.3 0.0 copy-start
  3.4 0.0 copy-start.1
  3.4 0.0 copy-start.2
  3.4 0.1 copy.12.eigvecs
  3.4 0.6 %copy-done = s32[48]{0:T(128)S(1)} copy-done((s32[48]{0:T(128)S(1)}, s32[48]{0:T(128)}, u32[]{:S(2)}) %copy-start) | copy-done | bytes 216
  4.0 0.0 copy-done.1
  4.0 0.0 copy-done.2
  4.0 37.0 %shard_map.86 = (f32[4,1,96]{2,1,0:T(1,128)S(1)}, f32[4,1,4]{2,1,0:T(1,128)S(1)}) custom-call(f32[8,1,1,6,256]{4,3,2,1,0:T(8,128)S(1)} %copy.9.noise, f32[4,3,1,1,6,256]{5,4,3,2,1,0:T(8,128)S(1)} %copy.10.gauge, f32[2,6,1,1,12,256]{5,4,3,2,1,0:T(8,128)S(1)} %copy.11.clover, f32[48,1,1,6,256]{4,3,2,1,0:T(8,128)S(1)} %copy.12.eigvecs, s32[48]{0:T(128)S(1)} %copy-done, ...), custom_call_target="tpu_custom_call" | custom-call | tf_op jit(solution)/shard_map/pallas_call | solution.py:309
  41.0 0.6 %copy.15 = f32[4,1,96]{2,1,0:T(1,128)} copy(f32[4,1,96]{2,1,0:T(1,128)S(1)} %get-tuple-element.4) | data formatting | bytes 3072
  41.6 0.6 %copy.16 = f32[4,1,4]{2,1,0:T(1,128)} copy(f32[4,1,4]{2,1,0:T(1,128)S(1)} %get-tuple-element.5) | data formatting | bytes 128
Async XLA Ops:
  0.6 2.7 %copy-start.3 = (f32[48,1,1,6,256]{4,2,3,1,0:T(1,128)S(1)}, f32[48,1,1,6,256]{4,2,3,1,0:T(1,128)}, u32[]{:S(2)}) copy-start(f32[48,1,1,6,256]{4,2,3,1,0:T(1,128)} %param.10) | copy-start | bytes 884740
  3.3 0.7 %copy-start = (s32[48]{0:T(128)S(1)}, s32[48]{0:T(128)}, u32[]{:S(2)}) copy-start(s32[48]{0:T(128)} %partner.1) | copy-start | bytes 580
  3.4 0.7 %copy-start.1 = (s32[8]{0:T(128)S(1)}, s32[8]{0:T(128)}, u32[]{:S(2)}) copy-start(s32[8]{0:T(128)} %dilution.1) | copy-start | bytes 100
  3.4 0.7 %copy-start.2 = (s32[4]{0:T(128)S(1)}, s32[4]{0:T(128)}, u32[]{:S(2)}) copy-start(s32[4]{0:T(128)} %boundary.1) | copy-start | bytes 52

commit v2 on v1

v2 whole, which is shorter than its diff:
```python
import functools
import math

import jax
import jax.numpy as jnp
from jax import lax
from jax.experimental import pallas as pl
from jax.experimental.pallas import tpu as pltpu
from jax.sharding import PartitionSpec as P

ITERS = 4
DILUTE = 4
GROUPS = 2
MESH = pl.DeviceIdType.MESH

diag_term = 4.1
step_size = 0.2
twist_table = (
    (((1, 0, -1), (0, 0, -1)), ((1, 0, 1), (0, 0, 1))),
    (((1, -1, 0), (0, 1, 0)), ((1, 1, 0), (0, -1, 0))),
    (((0, 0, -1), (1, 0, 1)), ((0, 0, 1), (1, 0, -1))),
    (((0, 1, 0), (1, 1, 0)), ((0, 1, 0), (1, 1, 0))),
)


def signed_add(total, sign, value):
    return total + value if sign > 0 else total - value


def twist_terms(real_coef, imag_coef, real, imag):
    if imag_coef == 0:
        return (real_coef, real), (real_coef, imag)
    return (-imag_coef, imag), (imag_coef, real)


def kernel(
    times, planes, noise_in, gauge_in, clover_in, eig_in, partner_in, dilution_in, boundary_in,
    per_out, cor_out,
    noise, gauge, clover, eigvecs, partner, dilution, boundary,
    links, clov, src, sol, acc, first_out, first_in, sbuf, rbuf, eig_hi, eig_lo,
    part, red, own, gat, onehot,
    load_sem, first_ssem, first_rsem, ssem, rsem, red_ssem, red_rsem, gat_ssem, gat_rsem,
):
    loads = []
    pairs = (
        (boundary_in, boundary), (dilution_in, dilution), (noise_in, noise), (gauge_in, gauge),
        (clover_in, clover), (eig_in, eigvecs), (partner_in, partner),
    )
    for k, (origin, target) in enumerate(pairs):
        loads.append(pltpu.make_async_copy(origin, target, load_sem.at[k]))
        loads[k].start()

    t_me = lax.axis_index("tm")
    z_me = lax.axis_index("space")
    t_up, t_down = lax.rem(t_me + 1, times), lax.rem(t_me + times - 1, times)
    z_up, z_down = lax.rem(z_me + 1, planes), lax.rem(z_me + planes - 1, planes)

    barrier = pltpu.get_barrier_semaphore()
    for off in range(1, times):
        pl.semaphore_signal(
            barrier, inc=1, device_id={"tm": lax.rem(t_me + off, times)}, device_id_type=MESH
        )
    for off in range(1, planes):
        pl.semaphore_signal(
            barrier, inc=1, device_id={"space": lax.rem(z_me + off, planes)}, device_id_type=MESH
        )

    nsrc, sites = noise.shape[0], noise.shape[-1]
    group, width = nsrc // GROUPS, sites // GROUPS
    side = math.isqrt(sites)
    nev = eigvecs.shape[0]
    row = (1, sites)
    lane = lax.broadcasted_iota(jnp.int32, row, 1)
    x_row, y_row = lax.rem(lane, side), lax.div(lane, side)
    field = (nsrc, width)
    field_row = lax.broadcasted_iota(jnp.int32, field, 0)
    lower = field_row < group

    def spread(value):
        shape = value.shape[:-2] + field
        first = jnp.broadcast_to(value[..., :width], shape)
        second = jnp.broadcast_to(value[..., width:], shape)
        return jnp.where(jnp.broadcast_to(lower, shape), first, second)

    for k in range(4):
        loads[k].wait()
    phases = [1.0 - 2.0 * boundary[mu].astype(jnp.float32) for mu in range(4)]
    half_step = 0.5 * step_size
    one = jnp.ones(row, jnp.float32)
    signs = (
        jnp.where(x_row == side - 1, phases[0], one) * half_step,
        jnp.where(y_row == side - 1, phases[1], one) * half_step,
        jnp.where(z_me == planes - 1, phases[2], 1.0) * half_step * one,
        jnp.where(t_me == times - 1, phases[3], 1.0) * half_step * one,
    )

    def set_links(mu):
        for col in range(3):
            for p in range(2):
                value = gauge[mu, :, 2 * col + p] * signs[mu][None]
                links[mu, p, :, col] = spread(value)

    t_mod = lax.rem(t_me, DILUTE)
    spin_rows = []
    for g in range(GROUPS):
        source_row = lax.rem(field_row, group) + g * group
        spin_rows.append(lax.rem(source_row, 4))
        weight = jnp.zeros(field, jnp.float32)
        for j in range(g * group, (g + 1) * group):
            chosen = jnp.where(dilution[j] == t_mod, step_size, 0.0)
            weight = jnp.where(source_row == j, chosen, weight)
        for color in range(3):
            for p in range(2):
                k = 2 * color + p
                rows = []
                for y_half in range(GROUPS):
                    for j in range(g * group, (g + 1) * group):
                        rows.append(noise[j, k, :, y_half * width : (y_half + 1) * width])
                value = jnp.concatenate(rows, 0) * weight
                for d in (0, 2):
                    first_out[g, d, p, color] = value

    def expand(g, value):
        return jnp.stack([jnp.where(spin_rows[g] == s, value, 0.0) for s in range(4)])

    def half(mu, sign, re, im):
        real, imag = [], []
        for h in range(2):
            pick, rc, ic = twist_table[mu][0][h]
            tr, ti = twist_terms(rc, ic, re[2 + pick], im[2 + pick])
            real.append(signed_add(re[h], sign * tr[0], tr[1]))
            imag.append(signed_add(im[h], sign * ti[0], ti[1]))
        return jnp.stack(real), jnp.stack(imag)

    def forward(mu, vr, vi):
        real = imag = None
        for c in range(3):
            ur, ui = links[mu, 0, :, c][None], links[mu, 1, :, c][None]
            ar, ai = vr[:, c : c + 1], vi[:, c : c + 1]
            dr, di = ur * ar - ui * ai, ur * ai + ui * ar
            real, imag = (dr, di) if c == 0 else (real + dr, imag + di)
        return real, imag

    def adjoint(mu, vr, vi):
        real = imag = None
        for c in range(3):
            ur, ui = links[mu, 0, c][None], links[mu, 1, c][None]
            ar, ai = vr[:, c : c + 1], vi[:, c : c + 1]
            dr, di = ur * ar + ui * ai, ur * ai - ui * ar
            real, imag = (dr, di) if c == 0 else (real + dr, imag + di)
        return real, imag

    def gather_in(g, mu, ahead, behind):
        diff = (behind[0] - ahead[0], behind[1] - ahead[1])
        for p in range(2):
            acc[g, p, 0:2] += ahead[p] + behind[p]
        for h in range(2):
            pick, rc, ic = twist_table[mu][1][h]
            terms = twist_terms(rc, ic, diff[0][pick], diff[1][pick])
            for p in range(2):
                acc[g, p, 2 + h] = signed_add(acc[g, p, 2 + h], terms[p][0], terms[p][1])

    flat = (6 * nsrc, width)
    flat_lane = lax.broadcasted_iota(jnp.int32, flat, 1)
    flat_x = lax.rem(flat_lane, side)
    edge = (6, nsrc, width)
    edge_lane = lax.broadcasted_iota(jnp.int32, edge, 2)

    def shift(mu, ahead, value):
        value = value.reshape(flat)
        if mu == 0:
            if ahead:
                moved = jnp.where(
                    flat_x == side - 1,
                    pltpu.roll(value, side - 1, 1),
                    pltpu.roll(value, width - 1, 1),
                )
            else:
                moved = jnp.where(
                    flat_x == 0,
                    pltpu.roll(value, width - side + 1, 1),
                    pltpu.roll(value, 1, 1),
                )
        else:
            moved = pltpu.roll(value, width - side if ahead else side, 1).reshape(edge)
            other = jnp.concatenate([moved[:, group:], moved[:, :group]], 1)
            moved = jnp.where(
                edge_lane >= width - side if ahead else edge_lane < side, other, moved
            )
        return moved.reshape(2, 3, nsrc, width)

    targets = ({"tm": t_down}, {"tm": t_up}, {"space": z_down}, {"space": z_up})

    def first_copy(g, d):
        return pltpu.make_async_remote_copy(
            src_ref=first_out.at[g, d],
            dst_ref=first_in.at[g, d],
            send_sem=first_ssem.at[g, d],
            recv_sem=first_rsem.at[g, d],
            device_id=targets[d],
            device_id_type=MESH,
        )

    def copy(g, it, d):
        return pltpu.make_async_remote_copy(
            src_ref=sbuf.at[g, it, d],
            dst_ref=rbuf.at[g, it, d],
            send_sem=ssem.at[g, it, d],
            recv_sem=rsem.at[g, it, d],
            device_id=targets[d],
            device_id_type=MESH,
        )

    def send(g, it):
        re, im = sol[g, 0], sol[g, 1]
        for mu, d in ((3, 0), (2, 2)):
            sbuf[g, it, d, 0], sbuf[g, it, d, 1] = half(mu, -1, re, im)
            copy(g, it, d).start()
            behind = adjoint(mu, *half(mu, 1, re, im))
            sbuf[g, it, d + 1, 0], sbuf[g, it, d + 1, 1] = behind
            copy(g, it, d + 1).start()

    def local(g):
        keep = 1.0 - step_size * diag_term
        for h in range(2):
            real = imag = None
            for b in range(6):
                cr, ci = clov[h, 0, :, b], clov[h, 1, :, b]
                vr = sol[g, 0, 2 * h + b // 3, b % 3][None]
                vi = sol[g, 1, 2 * h + b // 3, b % 3][None]
                dr, di = cr * vr - ci * vi, cr * vi + ci * vr
                real, imag = (dr, di) if b == 0 else (real + dr, imag + di)
            for p, value in enumerate((real, imag)):
                lo = 2 * h
                acc[g, p, lo : lo + 2] = (
                    value.reshape(2, 3, nsrc, width)
                    + keep * sol[g, p, lo : lo + 2]
                    + src[g, p, lo : lo + 2]
                )
        re, im = sol[g, 0], sol[g, 1]
        for mu in range(2):
            ahead = half(mu, -1, re, im)
            ahead = forward(mu, shift(mu, True, ahead[0]), shift(mu, True, ahead[1]))
            behind = adjoint(mu, *half(mu, 1, re, im))
            behind = (shift(mu, False, behind[0]), shift(mu, False, behind[1]))
            gather_in(g, mu, ahead, behind)

    def finish(g, it):
        for mu, d in ((2, 2), (3, 0)):
            copy(g, it, d).wait_recv()
            copy(g, it, d + 1).wait_recv()
            ahead = forward(mu, rbuf[g, it, d, 0], rbuf[g, it, d, 1])
            gather_in(g, mu, ahead, (rbuf[g, it, d + 1, 0], rbuf[g, it, d + 1, 1]))
        sol[g] = acc[g]

    def finish_first(g):
        for mu, d in ((2, 2), (3, 0)):
            first_copy(g, d).wait_recv()
            first_copy(g, d + 1).wait_recv()
            ahead = [expand(g, first_in[g, d, p]) for p in range(2)]
            ahead = forward(mu, *half(mu, -1, *ahead))
            behind = [expand(g, first_in[g, d + 1, p]) for p in range(2)]
            gather_in(g, mu, ahead, half(mu, 1, *behind))
        sol[g] = acc[g]

    for mu, d in ((3, 0), (2, 2)):
        set_links(mu)
        for g in range(GROUPS):
            pair = [first_out[g, d, p][None] for p in range(2)]
            re, im = adjoint(mu, *pair)
            first_out[g, d + 1, 0], first_out[g, d + 1, 1] = re[0], im[0]
        if mu == 3:
            pl.semaphore_wait(barrier, times + planes - 2)
        for g in range(GROUPS):
            first_copy(g, d).start()
            first_copy(g, d + 1).start()

    for g in range(GROUPS):
        for p in range(2):
            value = expand(g, first_out[g, 0, p])
            src[g, p] = value
            sol[g, p] = value
    set_links(0)
    set_links(1)
    loads[4].wait()
    for b in range(6):
        for p in range(2):
            clov[:, p, :, b] = spread(clover[:, :, 2 * b + p] * (-step_size))

    for g in range(GROUPS):
        local(g)
    for g in range(GROUPS):
        finish_first(g)
        send(g, 0)
        local(g)

    loads[5].wait()
    for color in range(3):
        real = eigvecs[:, 2 * color].reshape(nev, sites)
        imag = eigvecs[:, 2 * color + 1].reshape(nev, sites)
        for p, (top, bottom) in enumerate(((real, -imag), (imag, real))):
            lo = (2 * color + p) * sites
            whole = jnp.concatenate([top, bottom], 0)
            high = whole.astype(jnp.bfloat16)
            eig_hi[:, lo : lo + sites] = high
            eig_lo[:, lo : lo + sites] = (whole - high.astype(jnp.float32)).astype(jnp.bfloat16)
    loads[6].wait()
    out_lane = lax.broadcasted_iota(jnp.int32, (1, onehot.shape[1]), 1)
    for k in range(nev):
        for p in range(2):
            onehot[p * nev + k : p * nev + k + 1, :] = jnp.where(
                out_lane == partner[k] + p * nev, 1.0, 0.0
            )

    def iteration(it, carry):
        for g in range(GROUPS):
            finish(g, it)
            send(g, it + 1)
            local(g)
        return carry

    lax.fori_loop(0, ITERS - 2, iteration, 0)

    dims = (((1,), (1,)), ((), ()))
    for g in range(GROUPS):
        finish(g, ITERS - 2)
        pieces = []
        for color in range(3):
            for p in range(2):
                for y_half in range(GROUPS):
                    lo = y_half * group
                    rows = [sol[g, p, s, color, lo : lo + group, :] for s in range(4)]
                    pieces.append(jnp.concatenate(rows, 0))
        whole = jnp.concatenate(pieces, 1)
        high = whole.astype(jnp.bfloat16)
        low = (whole - high.astype(jnp.float32)).astype(jnp.bfloat16)
        eh, el = eig_hi[...], eig_lo[...]
        sums = lax.dot_general(high, eh, dims, preferred_element_type=jnp.float32)
        sums += lax.dot_general(high, el, dims, preferred_element_type=jnp.float32)
        sums += lax.dot_general(low, eh, dims, preferred_element_type=jnp.float32)
        for s in range(4):
            for j in range(group):
                k = group * s + j
                part[4 * (g * group + j) + s] = sums[k : k + 1, :]

    share = own.shape[0]

    def reduce_copy(off):
        dst = lax.rem(z_me + off, planes)
        return pltpu.make_async_remote_copy(
            src_ref=part.at[pl.ds(dst * share, share)],
            dst_ref=red.at[off - 1],
            send_sem=red_ssem.at[off - 1],
            recv_sem=red_rsem.at[off - 1],
            device_id={"space": dst},
            device_id_type=MESH,
        )

    def gather_copy(off):
        return pltpu.make_async_remote_copy(
            src_ref=own,
            dst_ref=gat.at[off - 1],
            send_sem=gat_ssem.at[off - 1],
            recv_sem=gat_rsem.at[off - 1],
            device_id={"tm": lax.rem(t_me + off, times)},
            device_id_type=MESH,
        )

    for off in range(1, planes):
        reduce_copy(off).start()
    total = part[pl.ds(z_me * share, share)]
    for off in range(1, planes):
        reduce_copy(off).wait_recv()
        total = total + red[off - 1]
    own[...] = total
    for off in range(1, times):
        gather_copy(off).start()
    per_out[...] = total
    weighted = jnp.dot(
        total.reshape(share, 2 * nev),
        onehot[...],
        preferred_element_type=jnp.float32,
        precision=lax.Precision.HIGHEST,
    ).reshape(share, 1, 2 * nev)
    slot = lax.broadcasted_iota(jnp.int32, (share, 1, times), 2)
    value = jnp.sum(weighted * total, axis=-1, keepdims=True)
    result = jnp.where(slot == t_me, value, 0.0)
    for off in range(1, times):
        gather_copy(off).wait_recv()
        value = jnp.sum(weighted * gat[off - 1], axis=-1, keepdims=True)
        result = jnp.where(slot == lax.rem(t_me + times - off, times), value, result)
    cor_out[...] = result
    for off in range(1, planes):
        reduce_copy(off).wait_send()
    for off in range(1, times):
        gather_copy(off).wait_send()
    for g in range(GROUPS):
        for d in range(4):
            first_copy(g, d).wait_send()
            for it in range(ITERS - 1):
                copy(g, it, d).wait_send()


def shards(times, planes, *args):
    noise, gauge, clover, eigvecs = args[:4]
    assert noise.shape[1] == noise.shape[2] == 1
    nsrc, sites, nev = noise.shape[0], noise.shape[-1], eigvecs.shape[0]
    rows = 4 * nsrc
    share = rows // planes
    depth = 6 * sites
    f32 = jnp.float32
    field = (nsrc, sites // GROUPS)
    args = (
        noise.reshape(nsrc, 6, 1, sites),
        gauge.reshape(4, 3, 6, 1, sites),
        clover.reshape(2, 6, 12, 1, sites),
        eigvecs.reshape(nev, 6, 1, sites),
    ) + args[4:]
    vmem = pl.BlockSpec(memory_space=pltpu.VMEM)
    dma = pltpu.SemaphoreType.DMA
    return pl.pallas_call(
        functools.partial(kernel, times, planes),
        out_shape=(
            jax.ShapeDtypeStruct((share, 1, 2 * nev), f32),
            jax.ShapeDtypeStruct((share, 1, times), f32),
        ),
        in_specs=[pl.BlockSpec(memory_space=pltpu.HBM)] * 7,
        out_specs=(vmem, vmem),
        scratch_shapes=[
            *[pltpu.VMEM(array.shape, f32) for array in args[:4]],
            *[pltpu.SMEM(array.shape, jnp.int32) for array in args[4:]],
            pltpu.VMEM((4, 2, 3, 3) + field, f32),
            pltpu.VMEM((2, 2, 6, 6) + field, f32),
            pltpu.VMEM((GROUPS, 2, 4, 3) + field, f32),
            pltpu.VMEM((GROUPS, 2, 4, 3) + field, f32),
            pltpu.VMEM((GROUPS, 2, 4, 3) + field, f32),
            pltpu.VMEM((GROUPS, 4, 2, 3) + field, f32),
            pltpu.VMEM((GROUPS, 4, 2, 3) + field, f32),
            pltpu.VMEM((GROUPS, ITERS - 1, 4, 2, 2, 3) + field, f32),
            pltpu.VMEM((GROUPS, ITERS - 1, 4, 2, 2, 3) + field, f32),
            pltpu.VMEM((2 * nev, depth), jnp.bfloat16),
            pltpu.VMEM((2 * nev, depth), jnp.bfloat16),
            pltpu.VMEM((rows, 1, 2 * nev), f32),
            pltpu.VMEM((planes - 1, share, 1, 2 * nev), f32),
            pltpu.VMEM((share, 1, 2 * nev), f32),
            pltpu.VMEM((times - 1, share, 1, 2 * nev), f32),
            pltpu.VMEM((2 * nev, 2 * nev), f32),
            dma((len(args),)),
            dma((GROUPS, 4)),
            dma((GROUPS, 4)),
            dma((GROUPS, ITERS - 1, 4)),
            dma((GROUPS, ITERS - 1, 4)),
            dma((planes - 1,)),
            dma((planes - 1,)),
            dma((times - 1,)),
            dma((times - 1,)),
        ],
        compiler_params=pltpu.CompilerParams(
            collective_id=0, has_side_effects=True, vmem_limit_bytes=32 * 1024 * 1024
        ),
    )(*args)


def solution(mesh):
    return jax.shard_map(
        functools.partial(shards, mesh.shape["tm"], mesh.shape["space"]),
        mesh=mesh,
        in_specs=(
            P(None, "tm", "space", None, None),
            P(None, None, "tm", "space", None, None),
            P(None, None, "tm", "space", None, None),
            P(None, "tm", "space", None, None),
            P(),
            P(),
            P(),
        ),
        out_specs=(P("space", "tm", None), P("space", "tm", None)),
        check_vma=False,
    )
```

time: 42.4 us -> 39.9 us (0.941)
  Pallas kernels: 37 us -> 33.5 us
  local copies, waits for them, and re-layouts: 4.5 us -> 5.37 us
    pallas_call x1, Pallas kernels: 37 us -> 33.5 us  [shards(): pl.pallas_call(functools.partial(kernel, times, planes), out_shape=(jax.S...]
    unnamed x14 -> x16, local copies, waits for them, and re-layouts: 4.5 us -> 5.37 us
where the time goes in v2:
time: 39.9 us; the launch traced here: 39.6 us
  Pallas kernels  33.5 us (84%)
  local copies, waits for them, and re-layouts  5.37 us (13%)
  between operations  0.67 us (2%)
    pallas_call x1, Pallas kernels, shards(): pl.pallas_call(functools.partial(kernel, times, planes), out_shape=(jax.S...  33.5 us
    unnamed x16, local copies, waits for them, and re-layouts  5.37 us

profile of v2, /device:TPU:0, one launch (start us, length us, event | category | flops | bytes accessed | tf_op | source)
XLA Modules:
  0.0 39.6 jit_solution(4113920007539927219)
XLA Ops:
  0.6 0.0 copy-start.4
  0.6 0.0 copy-start.5
  0.7 0.0 copy-start.6
  0.7 0.6 %copy-done.4 = s32[48]{0:T(128)S(1)} copy-done((s32[48]{0:T(128)S(1)}, s32[48]{0:T(128)}, u32[]{:S(2)}) %copy-start.4) | copy-done | bytes 216
  1.3 0.0 copy-done.5
  1.3 0.0 copy-done.6
  1.3 0.0 copy-start
  1.3 1.0 %copy-done = f32[48,1,1,6,256]{4,2,3,1,0:T(1,128)S(1)} copy-done((f32[48,1,1,6,256]{4,2,3,1,0:T(1,128)S(1)}, f32[48,1,1,6,256]{4,2,3,1,0:T(1,128)}, u32[]{:S(2)}) %copy-start) | copy-done | bytes 294936
  2.3 0.0 copy-start.1
  2.3 0.9 %copy-done.1 = f32[2,6,1,1,12,256]{5,3,4,2,1,0:T(1,128)S(1)} copy-done((f32[2,6,1,1,12,256]{5,3,4,2,1,0:T(1,128)S(1)}, f32[2,6,1,1,12,256]{5,3,4,2,1,0:T(1,128)}, u32[]{:S(2)}) %copy-start.1) | copy-done | bytes 147480
  3.2 0.0 copy-start.2
  3.2 0.9 %copy-done.2 = f32[4,3,1,1,6,256]{5,3,4,2,1,0:T(1,128)S(1)} copy-done((f32[4,3,1,1,6,256]{5,3,4,2,1,0:T(1,128)S(1)}, f32[4,3,1,1,6,256]{5,3,4,2,1,0:T(1,128)}, u32[]{:S(2)}) %copy-start.2) | copy-done | bytes 73752
  4.1 0.0 copy-start.3
  4.1 0.8 %copy-done.3 = f32[8,1,1,6,256]{4,2,3,1,0:T(1,128)S(1)} copy-done((f32[8,1,1,6,256]{4,2,3,1,0:T(1,128)S(1)}, f32[8,1,1,6,256]{4,2,3,1,0:T(1,128)}, u32[]{:S(2)}) %copy-start.3) | copy-done | bytes 49176
  4.9 33.5 %shard_map.86 = (f32[4,1,96]{2,1,0:T(1,128)S(1)}, f32[4,1,4]{2,1,0:T(1,128)S(1)}) custom-call(f32[8,6,1,256]{3,2,1,0:T(1,128)S(1)} %bitcast.7, f32[4,3,6,1,256]{4,3,2,1,0:T(1,128)S(1)} %bitcast.6, f32[2,6,12,1,256]{4,3,2,1,0:T(1,128)S(1)} %bitcast.5, f32[48,6,1,256]{3,2,1,0:T(1,128)S(1)} %bitcast.4, s32[48]{0:T(128)S(1)} %copy-done.4, s32[8]{0:T(128)S(1)} %copy-done.5, ...), custom_call_target="tpu_custom_call" | custom-call | tf_op jit(solution)/shard_map/pallas_call | solution.py:421
  38.4 0.6 %copy.11 = f32[4,1,96]{2,1,0:T(1,128)} copy(f32[4,1,96]{2,1,0:T(1,128)S(1)} %get-tuple-element.4) | data formatting | bytes 3072
  39.0 0.6 %copy.12 = f32[4,1,4]{2,1,0:T(1,128)} copy(f32[4,1,4]{2,1,0:T(1,128)S(1)} %get-tuple-element.5) | data formatting | bytes 128
Async XLA Ops:
  0.6 0.7 %copy-start.4 = (s32[48]{0:T(128)S(1)}, s32[48]{0:T(128)}, u32[]{:S(2)}) copy-start(s32[48]{0:T(128)} %partner_in.1) | copy-start | bytes 580
  0.6 0.7 %copy-start.5 = (s32[8]{0:T(128)S(1)}, s32[8]{0:T(128)}, u32[]{:S(2)}) copy-start(s32[8]{0:T(128)} %dilution_in.1) | copy-start | bytes 100
  0.7 0.7 %copy-start.6 = (s32[4]{0:T(128)S(1)}, s32[4]{0:T(128)}, u32[]{:S(2)}) copy-start(s32[4]{0:T(128)} %boundary_in.1) | copy-start | bytes 52
  1.3 1.0 %copy-start = (f32[48,1,1,6,256]{4,2,3,1,0:T(1,128)S(1)}, f32[48,1,1,6,256]{4,2,3,1,0:T(1,128)}, u32[]{:S(2)}) copy-start(f32[48,1,1,6,256]{4,2,3,1,0:T(1,128)} %param.10) | copy-start | bytes 884740
  2.3 0.9 %copy-start.1 = (f32[2,6,1,1,12,256]{5,3,4,2,1,0:T(1,128)S(1)}, f32[2,6,1,1,12,256]{5,3,4,2,1,0:T(1,128)}, u32[]{:S(2)}) copy-start(f32[2,6,1,1,12,256]{5,3,4,2,1,0:T(1,128)} %param.9) | copy-start | bytes 442372
  3.2 0.9 %copy-start.2 = (f32[4,3,1,1,6,256]{5,3,4,2,1,0:T(1,128)S(1)}, f32[4,3,1,1,6,256]{5,3,4,2,1,0:T(1,128)}, u32[]{:S(2)}) copy-start(f32[4,3,1,1,6,256]{5,3,4,2,1,0:T(1,128)} %param.8) | copy-start | bytes 221188
  4.1 0.8 %copy-start.3 = (f32[8,1,1,6,256]{4,2,3,1,0:T(1,128)S(1)}, f32[8,1,1,6,256]{4,2,3,1,0:T(1,128)}, u32[]{:S(2)}) copy-start(f32[8,1,1,6,256]{4,2,3,1,0:T(1,128)} %param.7) | copy-start | bytes 147460

commit v3 on v2

--- a/solution.py
+++ b/solution.py
@@ -456,7 +456,7 @@
             dma((times - 1,)),
         ],
         compiler_params=pltpu.CompilerParams(
-            collective_id=0, has_side_effects=True, vmem_limit_bytes=32 * 1024 * 1024
+            collective_id=0, has_side_effects=True, vmem_limit_bytes=60 * 1024 * 1024
         ),
     )(*args)
 

time: 39.9 us -> 36.4 us (0.912)
  local copies, waits for them, and re-layouts: 5.37 us -> 1.89 us
    unnamed x16 -> x6, local copies, waits for them, and re-layouts: 5.37 us -> 1.89 us
where the time goes in v3:
time: 36.4 us; the launch traced here: 36.2 us
  Pallas kernels  33.7 us (93%)
  local copies, waits for them, and re-layouts  1.89 us (5%)
  between operations  0.65 us (2%)
    pallas_call x1, Pallas kernels, shards(): pl.pallas_call(functools.partial(kernel, times, planes), out_shape=(jax.S...  33.7 us
    unnamed x6, local copies, waits for them, and re-layouts  1.89 us

profile of v3, /device:TPU:0, one launch (start us, length us, event | category | flops | bytes accessed | tf_op | source)
XLA Modules:
  0.0 36.2 jit_solution(15471901263715826076)
XLA Ops:
  0.6 33.7 %shard_map.86 = (f32[4,1,96]{2,1,0:T(1,128)}, f32[4,1,4]{2,1,0:T(1,128)}) custom-call(f32[8,6,1,256]{3,2,1,0:T(1,128)} %bitcast.7, f32[4,3,6,1,256]{4,3,2,1,0:T(1,128)} %bitcast.6, f32[2,6,12,1,256]{4,3,2,1,0:T(1,128)} %bitcast.5, f32[48,6,1,256]{3,2,1,0:T(1,128)} %bitcast.4, s32[48]{0:T(128)} %partner_in.1, s32[8]{0:T(128)} %dilution_in.1, s32[4]{0:T(128)} %boundary_in.1), custom_call_target="tpu_custom_call" | custom-call | tf_op jit(solution)/shard_map/pallas_call | solution.py:421
  34.3 0.0 copy-start.1
  34.4 0.7 %copy-done.1 = f32[4,1,96]{2,1,0:T(1,128)S(1)} copy-done((f32[4,1,96]{2,1,0:T(1,128)S(1)}, f32[4,1,96]{2,1,0:T(1,128)}, u32[]{:S(2)}) %copy-start.1) | copy-done | bytes 1560
  35.0 0.0 copy-start
  35.0 0.6 %copy.11 = f32[4,1,96]{2,1,0:T(1,128)} copy(f32[4,1,96]{2,1,0:T(1,128)S(1)} %copy-done.1) | data formatting | bytes 3072
  35.6 0.1 copy-done
  35.7 0.6 %copy.12 = f32[4,1,4]{2,1,0:T(1,128)} copy(f32[4,1,4]{2,1,0:T(1,128)S(1)} %copy-done) | data formatting | bytes 128
Async XLA Ops:
  34.3 0.7 %copy-start.1 = (f32[4,1,96]{2,1,0:T(1,128)S(1)}, f32[4,1,96]{2,1,0:T(1,128)}, u32[]{:S(2)}) copy-start(f32[4,1,96]{2,1,0:T(1,128)} %get-tuple-element.4) | copy-start | bytes 4612
  35.0 0.7 %copy-start = (f32[4,1,4]{2,1,0:T(1,128)S(1)}, f32[4,1,4]{2,1,0:T(1,128)}, u32[]{:S(2)}) copy-start(f32[4,1,4]{2,1,0:T(1,128)} %get-tuple-element.5) | copy-start | bytes 196
